TPU v7x, 32 devices: a whole 2x2x4 slice. The times are simulated.
32 devices in a mesh: seq: 8 (over z, x), head: 4 (over y, core).
Axes of the slice: x: 2, y: 2, z: 4, core: 2. Of those that a mesh axis runs over, the one named last changes fastest.
Arguments:
- queries: bfloat16 [2048, 2048], P('seq', 'head'), may hold values from -180 to 180
- keys: bfloat16 [2048, 2048], P('seq', 'head'), may hold values from -7 to 7
- values: bfloat16 [2048, 2048], P('seq', 'head'), may hold values from -6 to 6
- out_grad: bfloat16 [2048, 2048], P('seq', 'head'), may hold values from -6 to 6
- rand_blocks: int32 [32, 3], replicated, may hold values from 0 to 31, as said below
- glob_blocks: int32 [8], P('seq'), may hold values from 0 to 31, as said below
Outputs:
- attn_out: bfloat16 [2048, 2048], P('seq', 'head')
- query_grad: bfloat16 [2048, 2048], P('seq', 'head')
- key_grad: bfloat16 [2048, 2048], P('seq', 'head')
- value_grad: bfloat16 [2048, 2048], P('seq', 'head')
Inputs may be any that keep to these rules, and one draw needn't show every extreme that they name: `rand_blocks`: rows 4 * i to 4 * (i + 1) - 1 are the query blocks of index i of seq. Among their 12 entries, the blocks of any one index j of seq (blocks 4 * j to 4 * (j + 1) - 1) are named at most 2 times; in every draw one index j is named exactly 2 times by the rows of every index i. `glob_blocks`: entry j is one of the blocks 4 * j to 4 * (j + 1) - 1.
All inputs are finite; a program needn't handle non-finite values.
Results may differ from a plain program's by a relative error of at most 0.0052.
Values may be sent and summed in bfloat16 or wider, within the bound.
A program may use at most 128 MiB of HBM per device.

v0:
```python
import math
import jax
import jax.numpy as jnp
from jax import lax
from jax.sharding import PartitionSpec as P

HDIM = 128
BLK = 64
GLEN = 16


def extended(array, sides, width):
    for axis, dim in sides:
        size, length = (lax.axis_size(axis), array.shape[dim])
        up = [(i, (i + 1) % size) for i in range(size - 1)]
        down = [(j, i) for i, j in up]
        last = lax.slice_in_dim(array, length - width, length, axis=dim)
        first = lax.slice_in_dim(array, 0, width, axis=dim)
        before = lax.ppermute(last, axis, up)
        after = lax.ppermute(first, axis, down)
        array = jnp.concatenate([before, array, after], axis=dim)
    return array


def shards(queries, keys, values, out_grad, rand_blocks, glob_blocks):
    rows_dev, width_dev = queries.shape
    head_count = width_dev // HDIM
    seq_count = lax.axis_size("seq")
    my_index = lax.axis_index("seq")
    blocks_dev = rows_dev // BLK
    total_blocks = blocks_dev * seq_count
    per_block = rand_blocks.shape[1]
    spots = blocks_dev * per_block
    capacity = max(2, (spots + seq_count - 1) // seq_count)
    scale = 1.0 / math.sqrt(HDIM)
    local_len = (3 + per_block) * BLK
    global_len = seq_count * GLEN
    paired = jnp.stack([keys, values], 1)
    padded = extended(paired, (("seq", 0),), BLK)
    earlier = padded[:rows_dev].reshape(blocks_dev, BLK, 2, width_dev)
    current = paired.reshape(blocks_dev, BLK, 2, width_dev)
    later = padded[2 * BLK :].reshape(blocks_dev, BLK, 2, width_dev)
    own_global = glob_blocks[0] - my_index * blocks_dev
    mine = lax.dynamic_slice_in_dim(paired, own_global * BLK, GLEN, 0)
    global_kv = lax.all_gather(mine, "seq", axis=0, tiled=True)
    plan = rand_blocks.reshape(seq_count, spots)
    owners = plan // blocks_dev
    targets = plan % blocks_dev
    member = (owners[:, :, None] == jnp.arange(seq_count, dtype=jnp.int32)[None, None, :]).astype(
        jnp.int32
    )
    ranks = jnp.sum(member * (jnp.cumsum(member, axis=1) - 1), axis=2)
    places = owners * capacity + ranks
    my_places = lax.dynamic_index_in_dim(places, my_index, 0, keepdims=False)
    asked = (
        (owners == my_index)[:, :, None]
        & (ranks[:, :, None] == jnp.arange(capacity, dtype=jnp.int32)[None, None, :])
    ).astype(jnp.int32)
    incoming = jnp.sum(asked * (targets[:, :, None] + 1), axis=1) - 1
    block_kv = paired.reshape(blocks_dev, BLK, 2, width_dev)
    outgoing = jnp.take(block_kv, jnp.maximum(incoming, 0), axis=0)
    received = lax.all_to_all(outgoing, "seq", split_axis=0, concat_axis=0, tiled=True)
    fetched = jnp.take(received.reshape(seq_count * capacity, BLK, 2, width_dev), my_places, axis=0)
    fetched = fetched.reshape(blocks_dev, per_block * BLK, 2, width_dev)
    local_kv = jnp.concatenate([earlier, current, later, fetched], 1)
    query_blocks = queries.reshape(blocks_dev, BLK, head_count, HDIM)
    grad_blocks = out_grad.reshape(blocks_dev, BLK, head_count, HDIM)
    local_keys = local_kv[:, :, 0].reshape(blocks_dev, local_len, head_count, HDIM)
    local_vals = local_kv[:, :, 1].reshape(blocks_dev, local_len, head_count, HDIM)
    global_keys = global_kv[:, 0].reshape(global_len, head_count, HDIM)
    global_vals = global_kv[:, 1].reshape(global_len, head_count, HDIM)
    block_ids = my_index * blocks_dev + jnp.arange(blocks_dev, dtype=jnp.int32)
    before_ok = jnp.broadcast_to((block_ids > 0)[:, None], (blocks_dev, BLK))
    after_ok = jnp.broadcast_to((block_ids < total_blocks - 1)[:, None], (blocks_dev, BLK))
    visible = jnp.concatenate(
        [
            before_ok,
            jnp.ones((blocks_dev, BLK), bool),
            after_ok,
            jnp.ones((blocks_dev, per_block * BLK), bool),
        ],
        1,
    )
    scores_local = (
        jnp.einsum("bqhd,bkhd->bhqk", query_blocks, local_keys, preferred_element_type=jnp.float32)
        * scale
    )
    scores_local = jnp.where(visible[:, None, None, :], scores_local, -jnp.inf)
    scores_global = (
        jnp.einsum("bqhd,khd->bhqk", query_blocks, global_keys, preferred_element_type=jnp.float32)
        * scale
    )
    top = jnp.maximum(
        jnp.max(scores_local, axis=-1, keepdims=True),
        jnp.max(scores_global, axis=-1, keepdims=True),
    )
    expo_local = jnp.exp(scores_local - top)
    expo_global = jnp.exp(scores_global - top)
    totals = jnp.sum(expo_local, axis=-1, keepdims=True) + jnp.sum(
        expo_global, axis=-1, keepdims=True
    )
    probs_local = expo_local / totals
    probs_global = expo_global / totals
    weights_local = probs_local.astype(jnp.bfloat16)
    weights_global = probs_global.astype(jnp.bfloat16)
    attended = jnp.einsum(
        "bhqk,bkhd->bqhd", weights_local, local_vals, preferred_element_type=jnp.float32
    ) + jnp.einsum(
        "bhqk,khd->bqhd", weights_global, global_vals, preferred_element_type=jnp.float32
    )
    attn_out = attended.reshape(rows_dev, width_dev).astype(jnp.bfloat16)
    dprobs_local = jnp.einsum(
        "bqhd,bkhd->bhqk", grad_blocks, local_vals, preferred_element_type=jnp.float32
    )
    dprobs_global = jnp.einsum(
        "bqhd,khd->bhqk", grad_blocks, global_vals, preferred_element_type=jnp.float32
    )
    delta = jnp.sum(probs_local * dprobs_local, axis=-1, keepdims=True) + jnp.sum(
        probs_global * dprobs_global, axis=-1, keepdims=True
    )
    dscores_local = (probs_local * (dprobs_local - delta) * scale).astype(jnp.bfloat16)
    dscores_global = (probs_global * (dprobs_global - delta) * scale).astype(jnp.bfloat16)
    query_sum = jnp.einsum(
        "bhqk,bkhd->bqhd", dscores_local, local_keys, preferred_element_type=jnp.float32
    ) + jnp.einsum(
        "bhqk,khd->bqhd", dscores_global, global_keys, preferred_element_type=jnp.float32
    )
    query_grad = query_sum.reshape(rows_dev, width_dev).astype(jnp.bfloat16)
    local_dk = jnp.einsum(
        "bhqk,bqhd->bkhd", dscores_local, query_blocks, preferred_element_type=jnp.float32
    )
    local_dv = jnp.einsum(
        "bhqk,bqhd->bkhd", weights_local, grad_blocks, preferred_element_type=jnp.float32
    )
    local_grads = jnp.stack(
        [
            local_dk.reshape(blocks_dev, local_len, width_dev),
            local_dv.reshape(blocks_dev, local_len, width_dev),
        ],
        2,
    )
    before_terms = local_grads[:, :BLK].reshape(rows_dev, 2, width_dev)
    here_terms = local_grads[:, BLK : 2 * BLK].reshape(rows_dev, 2, width_dev)
    after_terms = local_grads[:, 2 * BLK : 3 * BLK].reshape(rows_dev, 2, width_dev)
    rims = jnp.concatenate([before_terms[:BLK], after_terms[rows_dev - BLK :]], 0)
    rim_padded = extended(rims.astype(jnp.bfloat16), (("seq", 0),), BLK).astype(rims.dtype)
    window_sum = (
        here_terms
        + jnp.concatenate([before_terms[BLK:], rim_padded[3 * BLK :]], 0)
        + jnp.concatenate([rim_padded[:BLK], after_terms[: rows_dev - BLK]], 0)
    )
    slot_grads = local_grads[:, 3 * BLK :].reshape(spots, BLK * 2 * width_dev).astype(jnp.bfloat16)
    placing = (
        my_places[:, None] == jnp.arange(seq_count * capacity, dtype=jnp.int32)[None, :]
    ).astype(jnp.bfloat16)
    to_send = jnp.einsum(
        "ts,tx->sx", placing, slot_grads, preferred_element_type=jnp.float32
    ).astype(jnp.bfloat16)
    returned = lax.all_to_all(
        to_send.reshape(seq_count, capacity, BLK * 2 * width_dev),
        "seq",
        split_axis=0,
        concat_axis=0,
        tiled=True,
    )
    landing = (
        incoming.reshape(-1)[:, None] == jnp.arange(blocks_dev, dtype=jnp.int32)[None, :]
    ).astype(jnp.bfloat16)
    random_sum = jnp.einsum(
        "sn,sx->nx",
        landing,
        returned.reshape(seq_count * capacity, BLK * 2 * width_dev),
        preferred_element_type=jnp.float32,
    ).reshape(rows_dev, 2, width_dev)
    global_dk = jnp.einsum(
        "bhqk,bqhd->khd", dscores_global, query_blocks, preferred_element_type=jnp.float32
    )
    global_dv = jnp.einsum(
        "bhqk,bqhd->khd", weights_global, grad_blocks, preferred_element_type=jnp.float32
    )
    global_terms = jnp.stack(
        [global_dk.reshape(global_len, width_dev), global_dv.reshape(global_len, width_dev)], 1
    )
    summed_all = lax.psum(global_terms, "seq")
    own_term = lax.dynamic_slice_in_dim(summed_all, my_index * GLEN, GLEN, 0)
    combined = window_sum + random_sum
    base_rows = lax.dynamic_slice_in_dim(combined, own_global * BLK, GLEN, 0)
    combined = lax.dynamic_update_slice_in_dim(combined, base_rows + own_term, own_global * BLK, 0)
    key_grad = combined[:, 0].astype(jnp.bfloat16)
    value_grad = combined[:, 1].astype(jnp.bfloat16)
    return (attn_out, query_grad, key_grad, value_grad)


def solution(mesh):
    in_specs = (
        P("seq", "head"),
        P("seq", "head"),
        P("seq", "head"),
        P("seq", "head"),
        P(),
        P("seq"),
    )
    out_specs = (P("seq", "head"), P("seq", "head"), P("seq", "head"), P("seq", "head"))
    return jax.shard_map(shards, mesh=mesh, in_specs=in_specs, out_specs=out_specs, check_vma=False)
```

profile of v0, /device:TPU:0, one launch (start us, length us, event | category | flops | bytes accessed | tf_op | source)
XLA Modules:
  0.0 270.9 jit_solution(358742052973094636)
XLA Ops:
  13.8 7.4 %all-to-all-start = ((bf16[8,2,64,2,512]{4,2,3,1,0:T(8,128)(2,1)}), bf16[8,2,64,2,512]{4,2,3,1,0:T(8,128)(2,1)S(1)}, u32[]{:S(2)}, u32[]{:S(2)}) async-start(bf16[8,2,64,2,512]{4,2,3,1,0:T(8,128)(2,1)} %broadcast_select_fusion), calls=%async_computation | async-start | bytes 4194304 | tf_op jit(solution)/shard_map/all_to_all | solution.py:62
  21.9 4.6 %collective-permute-start = (bf16[64,2,512]{2,0,1:T(8,128)(2,1)}, bf16[64,2,512]{2,0,1:T(8,128)(2,1)}, u32[]{:S(2)}, u32[]{:S(2)}) collective-permute-start(bf16[64,2,512]{2,0,1:T(8,128)(2,1)} %get-tuple-element.20), channel_id=1, source_target_pairs={{0,4},{4,8},{8,12},{12,16},{16,20},{20,24},{24,28},{1,5},{5,9},{9,... | collective-permute-start | bytes 393224 | tf_op jit(solution)/shard_map/ppermute | solution.py:19
  31.7 61.0 %all_gather.3 = bf16[128,2,512]{2,1,0:T(2,128)(2,1)S(1)} all-gather(bf16[16,2,512]{2,1,0:T(2,128)(2,1)S(1)} %copy.241), channel_id=1, replica_groups=mesh['seq'=8,'head'=4] {'seq'}, dimensions={0}, use_global_device_ids=true | all-gather | bytes 294912 | tf_op jit(solution)/shard_map/all_gather | solution.py:45
  111.8 2.4 fusion.20
  114.3 2.7 copy.237
  118.1 3.7 %fusion.1 = (f32[4,4,64]{2,1,0:T(4,128)}, f32[4,4,384,64]{2,3,1,0:T(8,128)}) fusion(f32[4,4,64]{2,1,0:T(4,128)S(1)} %copy_add_fusion.1, f32[4,4,64]{2,1,0:T(4,128)S(1)} %copy_maximum_fusion, f32[4,4,384,64]{2,3,1,0:T(8,128)S(1)} %get-tuple-element.29, bf16[4,384,4,128]{1,3,2,0:T(8,128)(2,1)} %bitcast.176, bf16[4,64,4,128]{3,2,1,0:T(4,128)(2,1)S(1)} %copy-done.17), kind=kOutput, calls=%fused_computation.15 | convolution fusion | flops 102235136 | bytes 4993024 | tf_op jit(solution)/shard_map/bqhd,bkhd->bhqk/dot_general | solution.py:112
  121.9 2.4 copy.267
  126.4 2.4 fusion.4
  128.8 2.3 fusion.28
  131.1 3.5 %copy.266 = f32[4,384,1,512]{3,1,2,0:T(8,128)} copy(f32[4,384,1,512]{1,3,0,2:T(8,128)} %bitcast.154) | data formatting | bytes 6291456 | tf_op jit(solution)/shard_map/stack;reshape | solution.py:135
  134.7 2.3 fusion
  138.6 2.8 %copy.272 = bf16[4,192,2,512]{3,2,1,0:T(2,128)(2,1)} copy(bf16[4,192,2,512]{3,1,2,0:T(8,128)(2,1)S(1)} %slice.123) | data formatting | bytes 3145728 | tf_op jit(solution)/shard_map/slice | solution.py:152
  141.5 5.7 %convert_element_type.59 = bf16[12,65536]{1,0:T(8,128)(2,1)} reshape(bf16[4,192,2,512]{3,2,1,0:T(2,128)(2,1)} %copy.272) | data formatting | bytes 3145728 | tf_op jit(solution)/shard_map/convert_element_type | solution.py:152
  147.2 3.8 %convolution_convert_fusion = bf16[16,65536]{1,0:T(8,128)(2,1)} fusion(bf16[12,65536]{1,0:T(8,128)(2,1)} %convert_element_type.59, s32[12]{0:T(128)} %get-tuple-element.24), kind=kOutput, calls=%fused_computation.2 | convolution fusion | flops 26214592 | bytes 3670064 | tf_op jit(solution)/shard_map/ts,tx->sx/dot_general | solution.py:156
  151.0 3.6 %reshape.224 = bf16[8,2,65536]{2,1,0:T(2,128)(2,1)} reshape(bf16[16,65536]{1,0:T(8,128)(2,1)} %convolution_convert_fusion) | data formatting | bytes 4194304 | tf_op jit(solution)/shard_map/reshape | solution.py:160
  154.6 4.4 %all-to-all-start.1 = ((bf16[8,2,65536]{2,1,0:T(2,128)(2,1)}), bf16[8,2,65536]{2,1,0:T(2,128)(2,1)}, u32[]{:S(2)}, u32[]{:S(2)}) async-start(bf16[8,2,65536]{2,1,0:T(2,128)(2,1)} %reshape.224), calls=%async_computation.1 | async-start | bytes 4194304 | tf_op jit(solution)/shard_map/all_to_all | solution.py:159
  168.0 2.9 %fusion.11 = bf16[4,64,4,128]{3,1,2,0:T(8,128)(2,1)S(1)} fusion(f32[4,64,4,128]{3,1,2,0:T(8,128)S(1)} %convolution_bitcast_fusion.2, bf16[4,384,4,128]{1,3,2,0:T(8,128)(2,1)} %bitcast.177, f32[4,4,384,64]{2,3,1,0:T(8,128)} %copy-done.2, f32[4,4,64]{2,1,0:T(4,128)S(1)} %copy_add_fusion.1, f32[4,4,64]{2,1,0:T(4,128)S(1)} %copy_maximum_fusion), kind=kOutput, calls=%fused_computation.33 | convolution fusion | flops 102105088 | bytes 3940352 | tf_op jit(solution)/shard_map/bhqk,bkhd->bqhd/dot_general | solution.py:106
  177.0 2.6 fusion.10
  182.7 3.8 %collective-permute-start.2 = (bf16[64,2,512]{2,0,1:T(8,128)(2,1)S(1)}, bf16[64,2,512]{2,0,1:T(8,128)(2,1)S(1)}, u32[]{:S(2)}, u32[]{:S(2)}) collective-permute-start(bf16[64,2,512]{2,0,1:T(8,128)(2,1)S(1)} %get-tuple-element.10), channel_id=1, source_target_pairs={{0,4},{4,8},{8,12},{12,16},{16,20},{20,24},{24,28},{1,5},{5,9},{9,... | collective-permute-start | bytes 393224 | tf_op jit(solution)/shard_map/ppermute | solution.py:19
  189.8 4.0 %collective-permute-done.3 = bf16[64,2,512]{2,0,1:T(8,128)(2,1)S(1)} collective-permute-done((bf16[64,2,512]{2,0,1:T(8,128)(2,1)S(1)}, bf16[64,2,512]{2,0,1:T(8,128)(2,1)S(1)}, u32[]{:S(2)}, u32[]{:S(2)}) %collective-permute-start.3) | collective-permute-done | bytes 131104 | tf_op jit(solution)/shard_map/ppermute | solution.py:20
  194.6 15.2 %all-to-all-done.1 = bf16[8,2,65536]{2,1,0:T(2,128)(2,1)} async-done(((bf16[8,2,65536]{2,1,0:T(2,128)(2,1)}), bf16[8,2,65536]{2,1,0:T(2,128)(2,1)}, u32[]{:S(2)}, u32[]{:S(2)}) %all-to-all-start.1) | async-done | bytes 2097184 | tf_op jit(solution)/shard_map/all_to_all | solution.py:159
  209.8 2.1 reshape.225
  213.4 2.4 reshape.226
  217.7 44.7 %all-reduce.2.cloned.1.call-done = f32[128,2,512]{2,0,1:T(8,128)} async-done(((f32[128,2,512]{2,0,1:T(8,128)}), f32[128,2,512]{2,0,1:T(8,128)}) %all-reduce.2.cloned.1.call-update) | async-done | bytes 524304 | tf_op jit(solution)/shard_map/psum | solution.py:184
  (151 shorter events, 63.3 us)
Async XLA Ops:
  13.8 7.4 %copy-start.8 = (bf16[256,512]{1,0:T(8,128)(2,1)S(1)}, bf16[256,512]{1,0:T(8,128)(2,1)}, u32[]{:S(2)}) copy-start(bf16[256,512]{1,0:T(8,128)(2,1)} %param.7) | copy-start | bytes 786436
  13.8 7.4 %copy-start.9 = (bf16[256,512]{1,0:T(8,128)(2,1)S(1)}, bf16[256,512]{1,0:T(8,128)(2,1)}, u32[]{:S(2)}) copy-start(bf16[256,512]{1,0:T(8,128)(2,1)} %param.8) | copy-start | bytes 786436
  13.8 88.7 %all-to-all-start = ((bf16[8,2,64,2,512]{4,2,3,1,0:T(8,128)(2,1)}), bf16[8,2,64,2,512]{4,2,3,1,0:T(8,128)(2,1)S(1)}, u32[]{:S(2)}, u32[]{:S(2)}) async-start(bf16[8,2,64,2,512]{4,2,3,1,0:T(8,128)(2,1)} %broadcast_select_fusion), calls=%async_computation | async-start | bytes 4194304 | tf_op jit(solution)/shard_map/all_to_all | solution.py:62
  21.1 8.9 %copy-start.20 = (bf16[256,512]{1,0:T(8,128)(2,1)S(1)}, bf16[256,512]{1,0:T(8,128)(2,1)}, u32[]{:S(2)}) copy-start(bf16[256,512]{1,0:T(8,128)(2,1)} %param.6) | copy-start | bytes 786436
  21.1 9.0 %copy-start.21 = (bf16[256,512]{1,0:T(8,128)(2,1)S(1)}, bf16[256,512]{1,0:T(8,128)(2,1)}, u32[]{:S(2)}) copy-start(bf16[256,512]{1,0:T(8,128)(2,1)} %param.9) | copy-start | bytes 786436
  21.9 78.6 %collective-permute-start = (bf16[64,2,512]{2,0,1:T(8,128)(2,1)}, bf16[64,2,512]{2,0,1:T(8,128)(2,1)}, u32[]{:S(2)}, u32[]{:S(2)}) collective-permute-start(bf16[64,2,512]{2,0,1:T(8,128)(2,1)} %get-tuple-element.20), channel_id=1, source_target_pairs={{0,4},{4,8},{8,12},{12,16},{16,20},{20,24},{24,28},{1,5},{5,9},{9,... | collective-permute-start | bytes 393224 | tf_op jit(solution)/shard_map/ppermute | solution.py:19
  26.5 74.1 %collective-permute-start.1 = (bf16[64,2,512]{2,0,1:T(8,128)(2,1)}, bf16[64,2,512]{2,0,1:T(8,128)(2,1)}, u32[]{:S(2)}, u32[]{:S(2)}) collective-permute-start(bf16[64,2,512]{2,0,1:T(8,128)(2,1)} %get-tuple-element.21), channel_id=1, source_target_pairs={{4,0},{8,4},{12,8},{16,12},{20,16},{24,20},{28,24},{5,1},{9,5},{13... | collective-permute-start | bytes 393224 | tf_op jit(solution)/shard_map/ppermute | solution.py:20
  30.2 65.9 %copy-start.15 = (bf16[4,64,4,128]{3,2,1,0:T(4,128)(2,1)}, bf16[4,64,4,128]{3,2,1,0:T(4,128)(2,1)S(1)}, u32[]{:S(2)}) copy-start(bf16[4,64,4,128]{3,2,1,0:T(4,128)(2,1)S(1)} %reshape.222) | copy-start | bytes 786436
  96.1 4.4 %copy-start.19 = (bf16[128,1,512]{0,2,1:T(8,128)(2,1)}, bf16[128,1,512]{0,2,1:T(8,128)(2,1)S(1)}, u32[]{:S(2)}) copy-start(bf16[128,1,512]{0,2,1:T(8,128)(2,1)S(1)} %copy.291) | copy-start | bytes 393220
  110.5 7.6 %copy-start.2 = (f32[4,4,384,64]{2,3,1,0:T(8,128)}, f32[4,4,384,64]{2,3,1,0:T(8,128)S(1)}, u32[]{:S(2)}) copy-start(f32[4,4,384,64]{2,3,1,0:T(8,128)S(1)} %get-tuple-element.29) | copy-start | bytes 4718596
  114.3 2.7 copy-start.5
  114.3 3.9 %copy-start.17 = (bf16[4,64,4,128]{3,2,1,0:T(4,128)(2,1)S(1)}, bf16[4,64,4,128]{3,2,1,0:T(4,128)(2,1)}, u32[]{:S(2)}) copy-start(bf16[4,64,4,128]{3,2,1,0:T(4,128)(2,1)} %copy-done.15) | copy-start | bytes 786436
  126.4 2.4 copy-start.22
  154.6 55.2 %all-to-all-start.1 = ((bf16[8,2,65536]{2,1,0:T(2,128)(2,1)}), bf16[8,2,65536]{2,1,0:T(2,128)(2,1)}, u32[]{:S(2)}, u32[]{:S(2)}) async-start(bf16[8,2,65536]{2,1,0:T(2,128)(2,1)} %reshape.224), calls=%async_computation.1 | async-start | bytes 4194304 | tf_op jit(solution)/shard_map/all_to_all | solution.py:159
  159.0 103.4 %all-reduce.2.cloned.1.call-start = ((), (), s32[]{:S(2)}) async-start(), calls=%async_computation.2 | async-start | bytes 1048576 | tf_op jit(solution)/shard_map/psum | solution.py:184
  168.0 3.9 %copy-start.10 = (f32[4,128,256]{1,2,0:S(1)}, f32[4,128,256]{1,2,0}, u32[]{:S(2)}) copy-start(f32[4,128,256]{1,2,0} %fusion.59) | copy-start | bytes 1572868
  168.0 3.9 %copy-start.11 = (f32[4,4,64,128]{3,2,0,1:T(8,128)S(1)}, f32[4,4,64,128]{3,2,0,1:T(8,128)}, u32[]{:S(2)}) copy-start(f32[4,4,64,128]{3,2,0,1:T(8,128)} %get-tuple-element.5) | copy-start | bytes 1572868
  168.0 3.9 %copy-start.23 = (f32[4,4,64]{2,0,1:T(4,128)S(1)}, f32[4,4,64]{2,0,1:T(4,128)}, u32[]{:S(2)}) copy-start(f32[4,4,64]{2,0,1:T(4,128)} %copy.260) | copy-start | bytes 12292
  173.0 3.7 %copy-start.14 = (bf16[4,4,64,128]{3,2,0,1:T(8,128)(2,1)S(1)}, bf16[4,4,64,128]{3,2,0,1:T(8,128)(2,1)}, u32[]{:S(2)}) copy-start(bf16[4,4,64,128]{3,2,0,1:T(8,128)(2,1)} %copy-done.13) | copy-start | bytes 786436
  177.0 3.5 %copy-start = (f32[4,384,1,512]{3,1,2,0:T(8,128)S(1)}, f32[4,384,1,512]{3,1,2,0:T(8,128)}, u32[]{:S(2)}) copy-start(f32[4,384,1,512]{3,1,2,0:T(8,128)} %copy.266) | copy-start | bytes 9437188
  182.7 7.1 %collective-permute-start.2 = (bf16[64,2,512]{2,0,1:T(8,128)(2,1)S(1)}, bf16[64,2,512]{2,0,1:T(8,128)(2,1)S(1)}, u32[]{:S(2)}, u32[]{:S(2)}) collective-permute-start(bf16[64,2,512]{2,0,1:T(8,128)(2,1)S(1)} %get-tuple-element.10), channel_id=1, source_target_pairs={{0,4},{4,8},{8,12},{12,16},{16,20},{20,24},{24,28},{1,5},{5,9},{9,... | collective-permute-start | bytes 393224 | tf_op jit(solution)/shard_map/ppermute | solution.py:19
  186.5 7.3 %collective-permute-start.3 = (bf16[64,2,512]{2,0,1:T(8,128)(2,1)S(1)}, bf16[64,2,512]{2,0,1:T(8,128)(2,1)S(1)}, u32[]{:S(2)}, u32[]{:S(2)}) collective-permute-start(bf16[64,2,512]{2,0,1:T(8,128)(2,1)S(1)} %get-tuple-element.11), channel_id=1, source_target_pairs={{4,0},{8,4},{12,8},{16,12},{20,16},{24,20},{28,24},{5,1},{9,5},{13... | collective-permute-start | bytes 393224 | tf_op jit(solution)/shard_map/ppermute | solution.py:20
  194.6 17.3 %copy-start.25 = (s32[16]{0:T(128)S(1)}, s32[16]{0:T(128)}, u32[]{:S(2)}) copy-start(s32[16]{0:T(128)} %sub.62) | copy-start | bytes 196
  213.4 2.4 copy-start.12
  (9 other events, 12.2 us)
Sparse Core Ops, SparseCore 0:
  176.9 85.3 all-reduce.1
where the time goes:
time: 272 us; the launch traced here: 271 us
  waiting for transfers between devices  63.9 us (23%)
  blocking collectives  61 us (22%)
  local copies, waits for them, and re-layouts  57.8 us (21%)
  matrix products  27.4 us (10%)
  other arithmetic  23 us (8%)
  starting transfers between devices  22.7 us (8%)
  between operations  15.2 us (6%)
    all_gather x1, blocking collectives, shards(): global_kv = lax.all_gather(mine, 'seq', axis=0, tiled=True)  61 us
    psum x1, waiting for transfers between devices, shards(): summed_all = lax.psum(global_terms, 'seq')  44.7 us
    all_to_all x1, waiting for transfers between devices, shards(): lax.all_to_all(to_send.reshape(seq_count, capacity, BLK * 2 * width_dev),...  15.2 us
    unnamed x57, local copies, waits for them, and re-layouts  8.55 us
    ppermute x2, starting transfers between devices, extended(): before = lax.ppermute(last, axis, up)  8.31 us
    all_to_all x1, starting transfers between devices, shards(): lax.all_to_all(outgoing, 'seq', split_axis=0, concat_axis=0, tiled=True)  7.38 us
    another operation x2, local copies, waits for them, and re-layouts, shards(): jnp.stack([local_dk.reshape(blocks_dev, local_len, width_dev), local_dv.r...  5.89 us
    convert_element_type x1, local copies, waits for them, and re-layouts, shards(): local_grads[:, 3 * BLK:].reshape(spots, BLK * 2 * width_dev)  5.73 us
  transfers between devices with their start and end apart: 7, of which 3 were waited for; matrix products, arithmetic and copies ran while one was open for 17% of the time, Pallas kernels for 0%

commit v1 on v0

--- a/solution.py
+++ b/solution.py
@@ -1,12 +1,36 @@
+import functools
 import math
 import jax
 import jax.numpy as jnp
 from jax import lax
 from jax.sharding import PartitionSpec as P
+from jax.lax import axis_index, axis_size, ppermute
 
 HDIM = 128
 BLK = 64
 GLEN = 16
+
+
+def corner_recover(z_in, dev_axis):
+    opened, item_now = (axis_size(dev_axis), axis_index(dev_axis))
+    answer = z_in.shape[0] // opened
+    q_next = list(z_in.shape)
+    q_next[0] = answer
+    w1 = q_next[0]
+    q_next[0] = w1 * opened
+    e_now = jnp.zeros(q_next, z_in.dtype)
+    for q in range(opened):
+        val = lax.dynamic_slice_in_dim(z_in, (item_now ^ q) * answer, answer, axis=0)
+        if q:
+            all_blocks = []
+            for dev in range(opened):
+                all_blocks.append((dev, dev ^ q))
+            val = ppermute(val, axis_name=dev_axis, perm=all_blocks)
+        e_now = lax.dynamic_update_slice_in_dim(e_now, val, (item_now ^ q) * w1, axis=0)
+    return e_now
+
+
+place_points = functools.partial(corner_recover, dev_axis="seq")
 
 
 def extended(array, sides, width):
@@ -59,7 +83,7 @@
     incoming = jnp.sum(asked * (targets[:, :, None] + 1), axis=1) - 1
     block_kv = paired.reshape(blocks_dev, BLK, 2, width_dev)
     outgoing = jnp.take(block_kv, jnp.maximum(incoming, 0), axis=0)
-    received = lax.all_to_all(outgoing, "seq", split_axis=0, concat_axis=0, tiled=True)
+    received = place_points(outgoing)
     fetched = jnp.take(received.reshape(seq_count * capacity, BLK, 2, width_dev), my_places, axis=0)
     fetched = fetched.reshape(blocks_dev, per_block * BLK, 2, width_dev)
     local_kv = jnp.concatenate([earlier, current, later, fetched], 1)

time: 272 us -> 275 us (1.011)
  blocking collectives: 61 us -> 31.6 us
  waiting for transfers between devices: 63.9 us -> 80.2 us
  starting transfers between devices: 22.7 us -> 29.8 us
  local copies, waits for them, and re-layouts: 57.8 us -> 64.7 us
    all_gather x1, blocking collectives: 61 us -> 31.6 us  [shards(): global_kv = lax.all_gather(mine, 'seq', axis=0, tiled=True)]
    ppermute x0 -> x7, waiting for transfers between devices: none -> 20 us  [corner_recover(): val = ppermute(val, axis_name=dev_axis, perm=all_blocks)]
    ppermute x0 -> x7, starting transfers between devices: none -> 13.6 us  [corner_recover(): val = ppermute(val, axis_name=dev_axis, perm=all_blocks)]
    all_to_all x1 -> x0, starting transfers between devices: 7.38 us -> none  [shards(): lax.all_to_all(outgoing, 'seq', split_axis=0, concat_axis=0, tiled=True)]
    psum x1, waiting for transfers between devices: 44.7 us -> 39.1 us  [shards(): summed_all = lax.psum(global_terms, 'seq')]
    dynamic_update_slice x0 -> x7, local copies, waits for them, and re-layouts: none -> 2.99 us  [corner_recover(): lax.dynamic_update_slice_in_dim(e_now, val, (item_now ^ q) * w1, axis=0)]
    unnamed x57 -> x67, local copies, waits for them, and re-layouts: 8.55 us -> 8.87 us
  transfers between devices with their start and end apart: 7 -> 13, of which waited for: 3 -> 7; matrix products, arithmetic and copies ran while one was open for 17% -> 21% of each run, Pallas kernels for 0% -> 0%
where the time goes in v1:
time: 275 us; the launch traced here: 273 us
  waiting for transfers between devices  80.2 us (29%)
  local copies, waits for them, and re-layouts  64.7 us (24%)
  blocking collectives  31.6 us (11%)
  starting transfers between devices  29.8 us (11%)
  matrix products  27.4 us (10%)
  other arithmetic  24.4 us (9%)
  between operations  15.4 us (6%)
    psum x1, waiting for transfers between devices, shards(): summed_all = lax.psum(global_terms, 'seq')  39.1 us
    all_gather x1, blocking collectives, shards(): global_kv = lax.all_gather(mine, 'seq', axis=0, tiled=True)  31.6 us
    ppermute x7, waiting for transfers between devices, corner_recover(): val = ppermute(val, axis_name=dev_axis, perm=all_blocks)  20 us
    all_to_all x1, waiting for transfers between devices, shards(): lax.all_to_all(to_send.reshape(seq_count, capacity, BLK * 2 * width_dev),...  16.9 us
    ppermute x7, starting transfers between devices, corner_recover(): val = ppermute(val, axis_name=dev_axis, perm=all_blocks)  13.6 us
    ppermute x2, starting transfers between devices, extended(): before = lax.ppermute(last, axis, up)  9.24 us
    unnamed x67, local copies, waits for them, and re-layouts  8.87 us
    another operation x2, local copies, waits for them, and re-layouts, shards(): jnp.stack([local_dk.reshape(blocks_dev, local_len, width_dev), local_dv.r...  5.88 us
  transfers between devices with their start and end apart: 13, of which 7 were waited for; matrix products, arithmetic and copies ran while one was open for 21% of the time, Pallas kernels for 0%

profile of v1, /device:TPU:0, one launch (start us, length us, event | category | flops | bytes accessed | tf_op | source)
XLA Modules:
  0.0 273.5 jit_solution(7377280141223135345)
XLA Ops:
  8.9 5.5 %collective-permute-start = (bf16[64,2,512]{2,0,1:T(8,128)(2,1)}, bf16[64,2,512]{2,0,1:T(8,128)(2,1)}, u32[]{:S(2)}, u32[]{:S(2)}) collective-permute-start(bf16[64,2,512]{2,0,1:T(8,128)(2,1)} %get-tuple-element.28), channel_id=1, source_target_pairs={{0,4},{4,8},{8,12},{12,16},{16,20},{20,24},{24,28},{1,5},{5,9},{9,... | collective-permute-start | bytes 393224 | tf_op jit(solution)/shard_map/ppermute | solution.py:43
  22.5 5.7 %collective-permute-start.8 = (bf16[1,2,64,2,512]{4,2,3,1,0:T(8,128)(2,1)}, bf16[1,2,64,2,512]{4,2,3,1,0:T(8,128)(2,1)}, u32[]{:S(2)}, u32[]{:S(2)}) collective-permute-start(bf16[1,2,64,2,512]{4,2,3,1,0:T(8,128)(2,1)} %get-tuple-element.14), channel_id=1, source_target_pairs={{0,28},{4,24},{8,20},{12,16},{16,12},{20,8},{24,4},{28,0},{1,29},{... | collective-permute-start | bytes 786440 | tf_op jit(solution)/shard_map/ppermute | solution.py:28
  32.7 31.6 %all_gather.3 = bf16[128,2,512]{2,1,0:T(2,128)(2,1)S(1)} all-gather(bf16[16,2,512]{2,1,0:T(2,128)(2,1)S(1)} %copy.241), channel_id=1, replica_groups=mesh['seq'=8,'head'=4] {'seq'}, dimensions={0}, use_global_device_ids=true | all-gather | bytes 294912 | tf_op jit(solution)/shard_map/all_gather | solution.py:69
  79.9 3.3 %collective-permute-start.5 = (bf16[1,2,64,2,512]{4,2,3,1,0:T(8,128)(2,1)}, bf16[1,2,64,2,512]{4,2,3,1,0:T(8,128)(2,1)S(1)}, u32[]{:S(2)}, u32[]{:S(2)}) collective-permute-start(bf16[1,2,64,2,512]{4,2,3,1,0:T(8,128)(2,1)} %get-tuple-element.17), channel_id=1, source_target_pairs={{0,16},{4,20},{8,24},{12,28},{16,0},{20,4},{24,8},{28,12},{1,17},{... | collective-permute-start | bytes 786440 | tf_op jit(solution)/shard_map/ppermute | solution.py:28
  89.2 14.8 %collective-permute-done.5 = bf16[1,2,64,2,512]{4,2,3,1,0:T(8,128)(2,1)S(1)} collective-permute-done((bf16[1,2,64,2,512]{4,2,3,1,0:T(8,128)(2,1)}, bf16[1,2,64,2,512]{4,2,3,1,0:T(8,128)(2,1)S(1)}, u32[]{:S(2)}, u32[]{:S(2)}) %collective-permute-start.5) | collective-permute-done | bytes 262176 | tf_op jit(solution)/shard_map/ppermute | solution.py:28
  104.0 3.0 %collective-permute-done.6 = bf16[1,2,64,2,512]{4,2,3,1,0:T(8,128)(2,1)S(1)} collective-permute-done((bf16[1,2,64,2,512]{4,2,3,1,0:T(8,128)(2,1)}, bf16[1,2,64,2,512]{4,2,3,1,0:T(8,128)(2,1)S(1)}, u32[]{:S(2)}, u32[]{:S(2)}) %collective-permute-start.6) | collective-permute-done | bytes 262176 | tf_op jit(solution)/shard_map/ppermute | solution.py:28
  117.8 2.4 fusion.20
  120.2 2.7 copy.237
  124.1 3.8 %fusion.1 = (f32[4,4,64]{2,1,0:T(4,128)}, f32[4,4,384,64]{2,3,1,0:T(8,128)}) fusion(f32[4,4,64]{2,1,0:T(4,128)S(1)} %copy_add_fusion.1, f32[4,4,64]{2,1,0:T(4,128)S(1)} %copy_maximum_fusion, f32[4,4,384,64]{2,3,1,0:T(8,128)S(1)} %get-tuple-element.37, bf16[4,384,4,128]{1,3,2,0:T(8,128)(2,1)} %bitcast.176, bf16[4,64,4,128]{3,2,1,0:T(4,128)(2,1)S(1)} %copy-done.17), kind=kOutput, calls=%fused_computation.15 | convolution fusion | flops 102235136 | bytes 4993024 | tf_op jit(solution)/shard_map/bqhd,bkhd->bhqk/dot_general | solution.py:136
  127.9 2.4 copy.267
  132.4 2.4 fusion.4
  134.8 2.3 fusion.28
  137.1 3.5 %copy.266 = f32[4,384,1,512]{3,1,2,0:T(8,128)} copy(f32[4,384,1,512]{1,3,0,2:T(8,128)} %bitcast.154) | data formatting | bytes 6291456 | tf_op jit(solution)/shard_map/stack;reshape | solution.py:159
  144.7 2.8 %copy.272 = bf16[4,192,2,512]{3,2,1,0:T(2,128)(2,1)} copy(bf16[4,192,2,512]{3,1,2,0:T(8,128)(2,1)S(1)} %slice.123) | data formatting | bytes 3145728 | tf_op jit(solution)/shard_map/slice | solution.py:176
  147.6 5.8 %convert_element_type.59 = bf16[12,65536]{1,0:T(8,128)(2,1)} reshape(bf16[4,192,2,512]{3,2,1,0:T(2,128)(2,1)} %copy.272) | data formatting | bytes 3145728 | tf_op jit(solution)/shard_map/convert_element_type | solution.py:176
  153.3 3.8 %convolution_convert_fusion = bf16[16,65536]{1,0:T(8,128)(2,1)} fusion(bf16[12,65536]{1,0:T(8,128)(2,1)} %convert_element_type.59, s32[12]{0:T(128)} %get-tuple-element.32), kind=kOutput, calls=%fused_computation.2 | convolution fusion | flops 26214592 | bytes 3670064 | tf_op jit(solution)/shard_map/ts,tx->sx/dot_general | solution.py:180
  157.1 3.6 %reshape.224 = bf16[8,2,65536]{2,1,0:T(2,128)(2,1)} reshape(bf16[16,65536]{1,0:T(8,128)(2,1)} %convolution_convert_fusion) | data formatting | bytes 4194304 | tf_op jit(solution)/shard_map/reshape | solution.py:184
  160.8 4.4 %all-to-all-start = ((bf16[8,2,65536]{2,1,0:T(2,128)(2,1)}), bf16[8,2,65536]{2,1,0:T(2,128)(2,1)}, u32[]{:S(2)}, u32[]{:S(2)}) async-start(bf16[8,2,65536]{2,1,0:T(2,128)(2,1)} %reshape.224), calls=%async_computation | async-start | bytes 4194304 | tf_op jit(solution)/shard_map/all_to_all | solution.py:183
  174.2 2.9 %fusion.11 = bf16[4,64,4,128]{3,1,2,0:T(8,128)(2,1)S(1)} fusion(f32[4,64,4,128]{3,1,2,0:T(8,128)S(1)} %convolution_bitcast_fusion.2, bf16[4,384,4,128]{1,3,2,0:T(8,128)(2,1)} %bitcast.177, f32[4,4,384,64]{2,3,1,0:T(8,128)} %copy-done.2, f32[4,4,64]{2,1,0:T(4,128)S(1)} %copy_add_fusion.1, f32[4,4,64]{2,1,0:T(4,128)S(1)} %copy_maximum_fusion), kind=kOutput, calls=%fused_computation.33 | convolution fusion | flops 102105088 | bytes 3940352 | tf_op jit(solution)/shard_map/bhqk,bkhd->bqhd/dot_general | solution.py:130
  183.2 2.6 fusion.10
  188.9 3.8 %collective-permute-start.9 = (bf16[64,2,512]{2,0,1:T(8,128)(2,1)S(1)}, bf16[64,2,512]{2,0,1:T(8,128)(2,1)S(1)}, u32[]{:S(2)}, u32[]{:S(2)}) collective-permute-start(bf16[64,2,512]{2,0,1:T(8,128)(2,1)S(1)} %get-tuple-element.10), channel_id=1, source_target_pairs={{0,4},{4,8},{8,12},{12,16},{16,20},{20,24},{24,28},{1,5},{5,9},{9,... | collective-permute-start | bytes 393224 | tf_op jit(solution)/shard_map/ppermute | solution.py:43
  196.3 3.9 %collective-permute-done.10 = bf16[64,2,512]{2,0,1:T(8,128)(2,1)S(1)} collective-permute-done((bf16[64,2,512]{2,0,1:T(8,128)(2,1)S(1)}, bf16[64,2,512]{2,0,1:T(8,128)(2,1)S(1)}, u32[]{:S(2)}, u32[]{:S(2)}) %collective-permute-start.10) | collective-permute-done | bytes 131104 | tf_op jit(solution)/shard_map/ppermute | solution.py:44
  201.0 16.9 %all-to-all-done = bf16[8,2,65536]{2,1,0:T(2,128)(2,1)} async-done(((bf16[8,2,65536]{2,1,0:T(2,128)(2,1)}), bf16[8,2,65536]{2,1,0:T(2,128)(2,1)}, u32[]{:S(2)}, u32[]{:S(2)}) %all-to-all-start) | async-done | bytes 2097184 | tf_op jit(solution)/shard_map/all_to_all | solution.py:183
  225.8 39.1 %all-reduce.2.cloned.1.call-done = f32[128,2,512]{2,0,1:T(8,128)} async-done(((f32[128,2,512]{2,0,1:T(8,128)}), f32[128,2,512]{2,0,1:T(8,128)}) %all-reduce.2.cloned.1.call-update) | async-done | bytes 524304 | tf_op jit(solution)/shard_map/psum | solution.py:208
  (182 shorter events, 85.4 us)
Async XLA Ops:
  8.9 67.2 %collective-permute-start = (bf16[64,2,512]{2,0,1:T(8,128)(2,1)}, bf16[64,2,512]{2,0,1:T(8,128)(2,1)}, u32[]{:S(2)}, u32[]{:S(2)}) collective-permute-start(bf16[64,2,512]{2,0,1:T(8,128)(2,1)} %get-tuple-element.28), channel_id=1, source_target_pairs={{0,4},{4,8},{8,12},{12,16},{16,20},{20,24},{24,28},{1,5},{5,9},{9,... | collective-permute-start | bytes 393224 | tf_op jit(solution)/shard_map/ppermute | solution.py:43
  14.3 62.3 %collective-permute-start.1 = (bf16[64,2,512]{2,0,1:T(8,128)(2,1)}, bf16[64,2,512]{2,0,1:T(8,128)(2,1)}, u32[]{:S(2)}, u32[]{:S(2)}) collective-permute-start(bf16[64,2,512]{2,0,1:T(8,128)(2,1)} %get-tuple-element.29), channel_id=1, source_target_pairs={{4,0},{8,4},{12,8},{16,12},{20,16},{24,20},{28,24},{5,1},{9,5},{13... | collective-permute-start | bytes 393224 | tf_op jit(solution)/shard_map/ppermute | solution.py:44
  21.2 11.4 %copy-start.8 = (bf16[256,512]{1,0:T(8,128)(2,1)S(1)}, bf16[256,512]{1,0:T(8,128)(2,1)}, u32[]{:S(2)}) copy-start(bf16[256,512]{1,0:T(8,128)(2,1)} %param.7) | copy-start | bytes 786436
  21.2 11.4 %copy-start.9 = (bf16[256,512]{1,0:T(8,128)(2,1)S(1)}, bf16[256,512]{1,0:T(8,128)(2,1)}, u32[]{:S(2)}) copy-start(bf16[256,512]{1,0:T(8,128)(2,1)} %param.8) | copy-start | bytes 786436
  21.2 43.0 %copy-start.20 = (bf16[256,512]{1,0:T(8,128)(2,1)S(1)}, bf16[256,512]{1,0:T(8,128)(2,1)}, u32[]{:S(2)}) copy-start(bf16[256,512]{1,0:T(8,128)(2,1)} %param.6) | copy-start | bytes 786436
  22.5 84.5 %collective-permute-start.8 = (bf16[1,2,64,2,512]{4,2,3,1,0:T(8,128)(2,1)}, bf16[1,2,64,2,512]{4,2,3,1,0:T(8,128)(2,1)}, u32[]{:S(2)}, u32[]{:S(2)}) collective-permute-start(bf16[1,2,64,2,512]{4,2,3,1,0:T(8,128)(2,1)} %get-tuple-element.14), channel_id=1, source_target_pairs={{0,28},{4,24},{8,20},{12,16},{16,12},{20,8},{24,4},{28,0},{1,29},{... | collective-permute-start | bytes 786440 | tf_op jit(solution)/shard_map/ppermute | solution.py:28
  28.2 55.9 %collective-permute-start.3 = (bf16[1,2,64,2,512]{4,2,3,1,0:T(8,128)(2,1)}, bf16[1,2,64,2,512]{4,2,3,1,0:T(8,128)(2,1)}, u32[]{:S(2)}, u32[]{:S(2)}) collective-permute-start(bf16[1,2,64,2,512]{4,2,3,1,0:T(8,128)(2,1)} %get-tuple-element.19), channel_id=1, source_target_pairs={{0,8},{4,12},{8,0},{12,4},{16,24},{20,28},{24,16},{28,20},{1,9},{5... | collective-permute-start | bytes 786440 | tf_op jit(solution)/shard_map/ppermute | solution.py:28
  28.2 51.7 %collective-permute-start.2 = (bf16[1,2,64,2,512]{4,2,3,1,0:T(8,128)(2,1)}, bf16[1,2,64,2,512]{4,2,3,1,0:T(8,128)(2,1)}, u32[]{:S(2)}, u32[]{:S(2)}) collective-permute-start(bf16[1,2,64,2,512]{4,2,3,1,0:T(8,128)(2,1)} %get-tuple-element.20), channel_id=1, source_target_pairs={{0,4},{4,0},{8,12},{12,8},{16,20},{20,16},{24,28},{28,24},{1,5},{5... | collective-permute-start | bytes 786440 | tf_op jit(solution)/shard_map/ppermute | solution.py:28
  65.4 7.2 %copy-start.15 = (bf16[4,64,4,128]{3,2,1,0:T(4,128)(2,1)}, bf16[4,64,4,128]{3,2,1,0:T(4,128)(2,1)S(1)}, u32[]{:S(2)}) copy-start(bf16[4,64,4,128]{3,2,1,0:T(4,128)(2,1)S(1)} %reshape.222) | copy-start | bytes 786436
  68.1 6.5 %copy-start.30 = (pred[4]{0:T(512)(128)(4,1)S(1)}, pred[4]{0:T(512)(128)(4,1)}, u32[]{:S(2)}) copy-start(pred[4]{0:T(512)(128)(4,1)} %get-tuple-element.40) | copy-start | bytes 16
  68.1 6.6 %copy-start.28 = (pred[384]{0:T(512)(128)(4,1)S(1)}, pred[384]{0:T(512)(128)(4,1)}, u32[]{:S(2)}) copy-start(pred[384]{0:T(512)(128)(4,1)} %pad.15.clone) | copy-start | bytes 1156
  68.1 6.6 %copy-start.29 = (pred[384]{0:T(512)(128)(4,1)S(1)}, pred[384]{0:T(512)(128)(4,1)}, u32[]{:S(2)}) copy-start(pred[384]{0:T(512)(128)(4,1)} %pad.13.clone) | copy-start | bytes 1156
  68.1 7.2 %copy-start.26 = (pred[4,3]{1,0:T(4,128)(4,1)S(1)}, pred[4,3]{1,0:T(4,128)(4,1)}, u32[]{:S(2)}) copy-start(pred[4,3]{1,0:T(4,128)(4,1)} %compare_and_fusion) | copy-start | bytes 40
  70.3 6.3 %copy-start.19 = (bf16[128,1,512]{0,2,1:T(8,128)(2,1)}, bf16[128,1,512]{0,2,1:T(8,128)(2,1)S(1)}, u32[]{:S(2)}) copy-start(bf16[128,1,512]{0,2,1:T(8,128)(2,1)S(1)} %copy.291) | copy-start | bytes 393220
  76.1 31.0 %collective-permute-start.7 = (bf16[1,2,64,2,512]{4,2,3,1,0:T(8,128)(2,1)}, bf16[1,2,64,2,512]{4,2,3,1,0:T(8,128)(2,1)S(1)}, u32[]{:S(2)}, u32[]{:S(2)}) collective-permute-start(bf16[1,2,64,2,512]{4,2,3,1,0:T(8,128)(2,1)} %get-tuple-element.15), channel_id=1, source_target_pairs={{0,24},{4,28},{8,16},{12,20},{16,8},{20,12},{24,0},{28,4},{1,25},{... | collective-permute-start | bytes 786440 | tf_op jit(solution)/shard_map/ppermute | solution.py:28
  76.6 12.5 %collective-permute-start.4 = (bf16[1,2,64,2,512]{4,2,3,1,0:T(8,128)(2,1)}, bf16[1,2,64,2,512]{4,2,3,1,0:T(8,128)(2,1)S(1)}, u32[]{:S(2)}, u32[]{:S(2)}) collective-permute-start(bf16[1,2,64,2,512]{4,2,3,1,0:T(8,128)(2,1)} %get-tuple-element.18), channel_id=1, source_target_pairs={{0,12},{4,8},{8,4},{12,0},{16,28},{20,24},{24,20},{28,16},{1,13},{... | collective-permute-start | bytes 786440 | tf_op jit(solution)/shard_map/ppermute | solution.py:28
  79.9 24.1 %collective-permute-start.5 = (bf16[1,2,64,2,512]{4,2,3,1,0:T(8,128)(2,1)}, bf16[1,2,64,2,512]{4,2,3,1,0:T(8,128)(2,1)S(1)}, u32[]{:S(2)}, u32[]{:S(2)}) collective-permute-start(bf16[1,2,64,2,512]{4,2,3,1,0:T(8,128)(2,1)} %get-tuple-element.17), channel_id=1, source_target_pairs={{0,16},{4,20},{8,24},{12,28},{16,0},{20,4},{24,8},{28,12},{1,17},{... | collective-permute-start | bytes 786440 | tf_op jit(solution)/shard_map/ppermute | solution.py:28
  84.1 22.9 %collective-permute-start.6 = (bf16[1,2,64,2,512]{4,2,3,1,0:T(8,128)(2,1)}, bf16[1,2,64,2,512]{4,2,3,1,0:T(8,128)(2,1)S(1)}, u32[]{:S(2)}, u32[]{:S(2)}) collective-permute-start(bf16[1,2,64,2,512]{4,2,3,1,0:T(8,128)(2,1)} %get-tuple-element.16), channel_id=1, source_target_pairs={{0,20},{4,16},{8,28},{12,24},{16,4},{20,0},{24,12},{28,8},{1,21},{... | collective-permute-start | bytes 786440 | tf_op jit(solution)/shard_map/ppermute | solution.py:28
  115.8 8.4 %copy-start.2 = (f32[4,4,384,64]{2,3,1,0:T(8,128)}, f32[4,4,384,64]{2,3,1,0:T(8,128)S(1)}, u32[]{:S(2)}) copy-start(f32[4,4,384,64]{2,3,1,0:T(8,128)S(1)} %get-tuple-element.37) | copy-start | bytes 4718596
  160.8 57.2 %all-to-all-start = ((bf16[8,2,65536]{2,1,0:T(2,128)(2,1)}), bf16[8,2,65536]{2,1,0:T(2,128)(2,1)}, u32[]{:S(2)}, u32[]{:S(2)}) async-start(bf16[8,2,65536]{2,1,0:T(2,128)(2,1)} %reshape.224), calls=%async_computation | async-start | bytes 4194304 | tf_op jit(solution)/shard_map/all_to_all | solution.py:183
  165.1 99.7 %all-reduce.2.cloned.1.call-start = ((), (), s32[]{:S(2)}) async-start(), calls=%async_computation.1 | async-start | bytes 1048576 | tf_op jit(solution)/shard_map/psum | solution.py:208
  188.9 7.4 %collective-permute-start.9 = (bf16[64,2,512]{2,0,1:T(8,128)(2,1)S(1)}, bf16[64,2,512]{2,0,1:T(8,128)(2,1)S(1)}, u32[]{:S(2)}, u32[]{:S(2)}) collective-permute-start(bf16[64,2,512]{2,0,1:T(8,128)(2,1)S(1)} %get-tuple-element.10), channel_id=1, source_target_pairs={{0,4},{4,8},{8,12},{12,16},{16,20},{20,24},{24,28},{1,5},{5,9},{9,... | collective-permute-start | bytes 393224 | tf_op jit(solution)/shard_map/ppermute | solution.py:43
  192.7 7.6 %collective-permute-start.10 = (bf16[64,2,512]{2,0,1:T(8,128)(2,1)S(1)}, bf16[64,2,512]{2,0,1:T(8,128)(2,1)S(1)}, u32[]{:S(2)}, u32[]{:S(2)}) collective-permute-start(bf16[64,2,512]{2,0,1:T(8,128)(2,1)S(1)} %get-tuple-element.11), channel_id=1, source_target_pairs={{4,0},{8,4},{12,8},{16,12},{20,16},{24,20},{28,24},{5,1},{9,5},{13... | collective-permute-start | bytes 393224 | tf_op jit(solution)/shard_map/ppermute | solution.py:44
  201.0 19.0 %copy-start.27 = (s32[16]{0:T(128)S(1)}, s32[16]{0:T(128)}, u32[]{:S(2)}) copy-start(s32[16]{0:T(128)} %sub.62) | copy-start | bytes 196
  (20 other events, 52.3 us)
Sparse Core Ops, SparseCore 0:
  183.1 81.7 all-reduce.1
